TPU v7x, 32 devices: a whole 2x2x4 slice. The times are simulated.
32 devices in a mesh: ta: 8 (over z, core), gz: 4 (over y, x).
Axes of the slice: x: 2, y: 2, z: 4, core: 2. Of those that a mesh axis runs over, the one named last changes fastest.
Arguments:
- source: bfloat16 [2, 4, 3, 8, 16, 512], P(None, None, None, 'ta', 'gz'), may hold values from -6 to 6
- gauge_links: bfloat16 [4, 2, 3, 3, 8, 16, 512], P(None, None, None, None, 'ta', 'gz'), may hold values from -2.5 to 2.5
- clover_diag: float32 [4, 3, 8, 16, 512], P(None, None, 'ta', 'gz'), may hold values from 0.5 to 4
- agg_map: int32 [8, 16, 512], P('ta', 'gz'), may hold values from 0 to 31
- prolong: bfloat16 [24, 2, 4, 3, 8, 16, 512], P(None, None, None, None, 'ta', 'gz'), may hold values from -0.078125 to 0.078125
- coarse_inverse: float32 [8, 768, 768], P('ta', 'gz'), may hold values from -16 to 16
Outputs:
- solution: float32 [2, 4, 3, 8, 16, 512], P(None, None, None, 'ta', 'gz')
Inputs may be any that keep to these rules, and one draw needn't show every extreme that they name: `agg_map`: aggregate numbers are local to each group of 4 devices along gz.
All inputs are finite; a program needn't handle non-finite values.
Results may differ from a plain program's by a relative error of at most 0.03.
Values may be sent and summed in bfloat16 or wider, within the bound.
A program may use at most 64 MiB of HBM per device.

v0:
```python
import jax
import jax.numpy as jnp
from jax import lax
from jax.sharding import PartitionSpec as P

LX = 32
LY = 16
NAGG = 32


mass_shift = -0.4
spin_perms = ((3, 2, 1, 0), (3, 2, 1, 0), (2, 3, 0, 1), (2, 3, 0, 1))
spin_real = (
    (0.0, 0.0, 0.0, 0.0),
    (-1.0, 1.0, 1.0, -1.0),
    (0.0, 0.0, 0.0, 0.0),
    (1.0, 1.0, 1.0, 1.0),
)
spin_imag = (
    (-1.0, -1.0, 1.0, 1.0),
    (0.0, 0.0, 0.0, 0.0),
    (-1.0, 1.0, 1.0, -1.0),
    (0.0, 0.0, 0.0, 0.0),
)


def shifted(block, axis, distance):
    devices = range(lax.axis_size(axis))
    route = [((i - distance) % len(devices), i) for i in devices]
    return lax.ppermute(block, axis, route)


def phase_mul(coef_re, coef_im, value_re, value_im):
    if coef_im == 0.0:
        return (coef_re * value_re, coef_re * value_im)
    return (-coef_im * value_im, coef_im * value_re)


def project(wide, direction, sign):
    rows_re = []
    rows_im = []
    for slot in range(2):
        other = spin_perms[direction][slot]
        term_re, term_im = phase_mul(
            spin_real[direction][slot], spin_imag[direction][slot], wide[0, other], wide[1, other]
        )
        rows_re.append(wide[0, slot] + sign * term_re)
        rows_im.append(wide[1, slot] + sign * term_im)
    return jnp.stack([jnp.stack(rows_re), jnp.stack(rows_im)])


def expand(half, direction, sign):
    rows_re = [None] * 4
    rows_im = [None] * 4
    for slot in range(2):
        other = spin_perms[direction][slot]
        rows_re[slot] = half[0, slot]
        rows_im[slot] = half[1, slot]
        term_re, term_im = phase_mul(
            spin_real[direction][other], spin_imag[direction][other], half[0, slot], half[1, slot]
        )
        rows_re[other] = sign * term_re
        rows_im[other] = sign * term_im
    return jnp.stack([jnp.stack(rows_re), jnp.stack(rows_im)])


def color_mix(link_pair, spinor, dagger):
    link_re = link_pair[0].astype(jnp.float32)
    link_im = link_pair[1].astype(jnp.float32)
    spin_re = spinor[0].astype(jnp.float32)
    spin_im = spinor[1].astype(jnp.float32)
    out_re = []
    out_im = []
    for row in range(3):
        acc_re = None
        acc_im = None
        for col in range(3):
            if dagger:
                entry_re = link_re[col, row]
                entry_im = -link_im[col, row]
            else:
                entry_re = link_re[row, col]
                entry_im = link_im[row, col]
            part_re = entry_re * spin_re[:, col] - entry_im * spin_im[:, col]
            part_im = entry_re * spin_im[:, col] + entry_im * spin_re[:, col]
            acc_re = part_re if acc_re is None else acc_re + part_re
            acc_im = part_im if acc_im is None else acc_im + part_im
        out_re.append(acc_re)
        out_im.append(acc_im)
    return jnp.stack([jnp.stack(out_re, axis=1), jnp.stack(out_im, axis=1)])


def local_shift(values, direction, step):
    dims_all = values.shape
    grid = values.reshape(dims_all[:-1] + (LY, LX))
    rolled = jnp.roll(grid, -step, axis=-1 if direction == 0 else -2)
    return rolled.reshape(dims_all)


def fwd_round(wide, direction):
    return lax.optimization_barrier(project(wide, direction, -1.0).astype(jnp.bfloat16))


def hopping(spinor, gauge_links):
    wide = spinor.astype(jnp.float32)
    total = jnp.zeros(spinor.shape, jnp.float32)
    back_space = lax.optimization_barrier(
        project(color_mix(gauge_links[2], spinor, True), 2, 1.0).astype(jnp.bfloat16)
    )
    back_time = lax.optimization_barrier(
        project(color_mix(gauge_links[3], spinor, True), 3, 1.0).astype(jnp.bfloat16)
    )
    send_bz = expand(back_space.astype(jnp.float32), 2, 1.0).astype(jnp.bfloat16)
    send_bt = expand(back_time.astype(jnp.float32), 3, 1.0).astype(jnp.bfloat16)
    ahead_time = shifted(spinor, "ta", -1)
    fwd_time = jnp.concatenate([spinor[:, :, :, 1:], ahead_time], axis=3)
    behind_time = shifted(send_bt, "ta", 1)
    bwd_time = jnp.concatenate([behind_time, send_bt[:, :, :, :-1]], axis=3)
    ahead_space = shifted(spinor[:, :, :, :, 0:1], "gz", -1)
    fwd_space = jnp.concatenate([spinor[:, :, :, :, 1:], ahead_space], axis=4)
    behind_space = shifted(send_bz[:, :, :, :, -1:], "gz", 1)
    bwd_space = jnp.concatenate([behind_space, send_bz[:, :, :, :, :-1]], axis=4)
    fwd_space = fwd_round(fwd_space.astype(jnp.float32), 2)
    fwd_time = fwd_round(fwd_time.astype(jnp.float32), 3)
    bwd_space = bwd_space[:, 0:2]
    bwd_time = bwd_time[:, 0:2]
    for direction in range(2):
        ahead = local_shift(fwd_round(wide, direction), direction, 1)
        total = total + expand(color_mix(gauge_links[direction], ahead, False), direction, -1.0)
        back_half = lax.optimization_barrier(
            project(color_mix(gauge_links[direction], spinor, True), direction, 1.0).astype(
                jnp.bfloat16
            )
        )
        behind = local_shift(back_half, direction, -1).astype(jnp.float32)
        total = total + expand(behind, direction, 1.0)
    total = total + expand(color_mix(gauge_links[2], fwd_space, False), 2, -1.0)
    total = total + expand(bwd_space.astype(jnp.float32), 2, 1.0)
    total = total + expand(color_mix(gauge_links[3], fwd_time, False), 3, -1.0)
    total = total + expand(bwd_time.astype(jnp.float32), 3, 1.0)
    return total


def shards(source, gauge_links, clover_diag, agg_map, prolong, coarse_inverse):
    highest = lax.Precision.HIGHEST
    diagonal = 4.0 + mass_shift + clover_diag
    source_wide = source.astype(jnp.float32)
    first_iter = source_wide / diagonal
    first_half = first_iter.astype(jnp.bfloat16)
    first_resid = source_wide - diagonal * first_iter + 0.5 * hopping(first_half, gauge_links)
    second_iter = first_iter + first_resid / diagonal
    second_half = second_iter.astype(jnp.bfloat16)
    second_resid = source_wide - diagonal * second_iter + 0.5 * hopping(second_half, gauge_links)
    resid_half = second_resid.astype(jnp.bfloat16)
    projected = jnp.einsum(
        "vrsctzn,rsctzn->vtzn", prolong, resid_half, preferred_element_type=jnp.float32
    )
    vectors = prolong.shape[0]
    labels = jnp.arange(NAGG, dtype=jnp.int32)
    member = agg_map.reshape(-1)[None, :] == labels[:, None]
    partial_sum = jnp.einsum(
        "am,vm->av", member.astype(jnp.float32), projected.reshape(vectors, -1), precision=highest
    )
    coarse_resid = lax.psum(partial_sum.reshape(-1), "gz")
    own_rows = jnp.dot(coarse_inverse[0], coarse_resid, precision=highest)
    correction = lax.all_gather(own_rows, "gz", axis=0, tiled=True)
    correction_half = correction.astype(jnp.bfloat16).reshape(NAGG, vectors)
    spread = jnp.einsum(
        "av,am->vm",
        correction_half,
        member.astype(jnp.bfloat16),
        preferred_element_type=jnp.float32,
    ).astype(jnp.bfloat16)
    smooth = jnp.einsum(
        "vrsctzn,vtzn->rsctzn",
        prolong,
        spread.reshape(projected.shape),
        preferred_element_type=jnp.float32,
    )
    return second_iter + smooth


def solution(mesh):
    return jax.shard_map(
        shards,
        mesh=mesh,
        in_specs=(
            P(None, None, None, "ta", "gz", None),
            P(None, None, None, None, "ta", "gz", None),
            P(None, None, "ta", "gz", None),
            P("ta", "gz", None),
            P(None, None, None, None, "ta", "gz", None),
            P("ta", "gz", None),
        ),
        out_specs=P(None, None, None, "ta", "gz", None),
        check_vma=False,
    )
```

profile of v0, /device:TPU:0, one launch (start us, length us, event | category | flops | bytes accessed | tf_op | source)
XLA Modules:
  0.0 72.3 jit_solution(8821755835692853902)
XLA Ops:
  0.0 1.0 %add_bitcast_fusion = f32[4,3,4,512]{3,2,1,0:T(4,128)S(1)} fusion(f32[4,3,1,4,512]{4,3,2,1,0:T(4,128)} %param.8), kind=kLoop, calls=%fused_computation.124 | loop fusion | flops 24576 | bytes 196608 | tf_op jit(solution)/shard_map/div | solution.py:148
  1.0 1.0 %fusion.281 = (f32[2,4,3,1,4,512]{5,4,2,3,1,0:T(4,128)S(1)}, bf16[2,4,3,1,4,512]{5,4,2,3,1,0:T(4,128)(2,1)S(1)}) fusion(f32[4,3,4,512]{3,2,1,0:T(4,128)S(1)} %add_bitcast_fusion, bf16[2,4,3,1,4,512]{5,4,3,2,1,0:T(4,128)(2,1)} %param.6), kind=kLoop, calls=%fused_computation.840 | loop fusion | flops 196608 | bytes 491520 | tf_op jit(solution)/shard_map/convert_element_type | solution.py:105
  1.9 4.5 %collective-permute-start.2 = (bf16[2,4,3,1,4,512]{5,4,2,3,1,0:T(4,128)(2,1)S(1)}, bf16[2,4,3,1,4,512]{5,4,2,3,1,0:T(4,128)(2,1)S(1)}, u32[]{:S(2)}, u32[]{:S(2)}) collective-permute-start(bf16[2,4,3,1,4,512]{5,4,2,3,1,0:T(4,128)(2,1)S(1)} %get-tuple-element.9), channel_id=1, source_target_pairs={{4,0},{8,4},{12,8},{16,12},{20,16},{24,20},{28,24},{0,28},{5,1},{9... | collective-permute-start | bytes 294920 | tf_op jit(solution)/shard_map/ppermute | solution.py:30
  6.5 0.7 slice.2542
  7.1 2.4 %collective-permute-start = (bf16[2,4,3,1,1,512]{5,4,2,3,1,0:T(2,128)(2,1)}, bf16[2,4,3,1,1,512]{5,4,2,3,1,0:T(2,128)(2,1)}, u32[]{:S(2)}, u32[]{:S(2)}) collective-permute-start(bf16[2,4,3,1,1,512]{5,4,2,3,1,0:T(2,128)(2,1)} %slice.2542), channel_id=1, source_target_pairs={{1,0},{2,1},{3,2},{0,3},{5,4},{6,5},{7,6},{4,7},{9,8},{10,9},{11,1... | collective-permute-start | bytes 73736 | tf_op jit(solution)/shard_map/ppermute | solution.py:30
  9.6 0.9 %bitcast_convert_fusion.9 = (f32[3,3,1,4,512]{4,3,1,0,2:T(4,128)S(1)}, f32[3,3,1,4,512]{4,3,1,0,2:T(4,128)S(1)}, f32[3,3,1,4,512]{4,3,1,0,2:T(4,128)S(1)}, f32[3...) fusion(bf16[4,2,3,3,1,4,512]{6,5,4,3,2,1,0:T(4,128)(2,1)} %param.7), kind=kLoop, calls=%fused_computation.204 | loop fusion | flops 147456 | bytes 884736 | tf_op jit(solution)/shard_map/convert_element_type | solution.py:68
  10.6 0.7 slice_bitcast_fusion.129
  11.6 0.3 copy-done.88
  12.4 0.7 fusion.39
  13.1 0.6 slice_bitcast_fusion.111
  14.7 0.2 reshape.7015
  14.8 0.1 slice.1197
  15.0 0.1 fusion.32
  15.1 0.1 reshape.7030
  15.2 0.1 reshape.7032
  15.7 0.3 copy-done.142
  16.7 0.2 reshape.7016
  16.9 0.1 slice.1244
  17.0 0.1 maximum_convert_fusion
  17.2 0.2 reshape.7035
  17.6 0.2 reshape.7017
  17.9 0.1 reshape.7037
  18.1 0.1 reshape.7039
  18.5 0.3 copy-done.160
  19.5 0.2 reshape.7018
  19.9 0.2 reshape.7040
  20.7 0.6 copy.342
  21.3 0.7 dynamic-slice
  22.7 0.9 %maximum_convert_fusion.4 = f32[2,4,3,1,4,512]{5,4,2,3,1,0:T(4,128)S(1)} fusion(bf16[2,4,3,1,1,512]{5,4,2,3,1,0:T(2,128)(2,1)} %collective-permute-done, bf16[2,4,3,1,3,512]{5,4,2,3,1,0:T(4,128)(2,1)S(1)} %slice.2541), kind=kLoop, calls=%fused_computation.78 | loop fusion | flops 196608 | bytes 294912 | tf_op jit(solution)/shard_map/convert_element_type | solution.py:123
  24.1 0.8 %fusion.43 = f32[2,2,3,1,4,512]{5,4,2,3,1,0:T(4,128)S(1)} fusion(bf16[2,4,3,1,1,512]{5,4,2,3,1,0:T(2,128)(2,1)} %collective-permute-done.1, bf16[1,4,3,1,4,512]{5,4,2,3,1,0:T(4,128)(2,1)S(1)} %maximum_bitcast_fusion.46, bf16[1,4,3,1,4,512]{5,4,2,3,1,0:T(4,128)(2,1)S(1)} %maximum_bitcast_fusion.45), kind=kLoop, calls=%fused_computation.138 | loop fusion | flops 147456 | bytes 221184 | tf_op jit(solution)/shard_map/convert_element_type | solution.py:138
  25.6 0.8 %slice_convert_fusion.1 = f32[2,2,3,1,4,512]{5,4,2,3,1,0:T(4,128)S(1)} fusion(bf16[2,4,3,1,4,512]{5,4,2,3,1,0:T(4,128)(2,1)} %collective-permute-done.3), kind=kLoop, calls=%fused_computation.136 | loop fusion | flops 24576 | bytes 147456 | tf_op jit(solution)/shard_map/convert_element_type | solution.py:140
  26.6 0.3 bitcast_convert_fusion.10
  27.3 0.2 reshape.7019
  27.5 0.1 slice.2661
  27.6 0.1 fusion.28
  27.7 0.1 reshape.7061
  27.9 0.1 reshape.7062
  29.0 0.2 reshape.7020
  29.1 0.1 slice.2691
  29.3 0.1 maximum_convert_fusion.2
  29.5 0.2 reshape.7065
  29.8 0.2 reshape.7021
  30.2 0.1 reshape.7066
  30.3 0.1 reshape.7067
  31.5 0.2 reshape.7022
  31.8 0.2 reshape.7068
  32.6 3.6 %collective-permute-start.6 = (bf16[2,4,3,1,4,512]{5,4,3,2,1,0:T(4,128)(2,1)S(1)}, bf16[2,4,3,1,4,512]{5,4,3,2,1,0:T(4,128)(2,1)S(1)}, u32[]{:S(2)}, u32[]{:S(2)}) collective-permute-start(bf16[2,4,3,1,4,512]{5,4,3,2,1,0:T(4,128)(2,1)S(1)} %get-tuple-element.6), channel_id=1, source_target_pairs={{4,0},{8,4},{12,8},{16,12},{20,16},{24,20},{28,24},{0,28},{5,1},{9... | collective-permute-start | bytes 294920 | tf_op jit(solution)/shard_map/ppermute | solution.py:30
  36.7 3.0 %collective-permute-start.4 = (bf16[2,4,3,1,1,512]{5,4,2,3,1,0:T(2,128)(2,1)S(1)}, bf16[2,4,3,1,1,512]{5,4,2,3,1,0:T(2,128)(2,1)S(1)}, u32[]{:S(2)}, u32[]{:S(2)}) collective-permute-start(bf16[2,4,3,1,1,512]{5,4,2,3,1,0:T(2,128)(2,1)S(1)} %slice.2726), channel_id=1, source_target_pairs={{1,0},{2,1},{3,2},{0,3},{5,4},{6,5},{7,6},{4,7},{9,8},{10,9},{11,1... | collective-permute-start | bytes 73736 | tf_op jit(solution)/shard_map/ppermute | solution.py:30
  40.3 0.2 collective-permute-start.7
  40.9 0.5 collective-permute-done.4
  42.0 2.9 %collective-permute-done.5 = bf16[2,4,3,1,1,512]{5,4,2,1,3,0:T(2,128)(2,1)S(1)} collective-permute-done((bf16[2,4,3,1,1,512]{5,4,2,1,3,0:T(2,128)(2,1)S(1)}, bf16[2,4,3,1,1,512]{5,4,2,1,3,0:T(2,128)(2,1)S(1)}, u32[]{:S(2)}, u32[]{:S(2)}) %collective-permute-start.5) | collective-permute-done | bytes 24608 | tf_op jit(solution)/shard_map/ppermute | solution.py:30
  45.7 0.7 collective-permute-done.7
  46.5 0.3 bitcast_convert_fusion
  46.9 0.2 copy-done.1
  47.0 1.3 %multiply_reduce_fusion.1 = f32[4,512,24]{1,0,2:T(4,128)S(1)} fusion(f32[4,512,3,2,4]{1,0,2,4,3:T(4,128)S(1)} %bitcast_convert_fusion, bf16[24,2,4,3,1,4,512]{6,5,4,3,2,1,0:T(4,128)(2,1)S(1)} %copy-done.1), kind=kLoop, calls=%fused_computation.1 | loop fusion | flops 3489792 | bytes 2752512
  48.3 1.3 %copy.331 = f32[4,512,24]{2,1,0:T(8,128)} copy(f32[4,512,24]{1,0,2:T(4,128)S(1)} %multiply_reduce_fusion.1) | data formatting | bytes 393216 | tf_op jit(solution)/shard_map/vrsctzn,rsctzn->vtzn/dot_general | solution.py:155
  49.6 1.7 %fusion.2 = f32[32,24]{1,0:T(8,128)S(1)} fusion(f32[24,2048]{0,1:T(8,128)} %bitcast.1396, s32[2048]{0:T(1024)S(1)} %bitcast.1413), kind=kOutput, calls=%fused_computation.10 | convolution fusion | flops 18939904 | bytes 207872 | tf_op jit(solution)/shard_map/am,vm->av/dot_general | solution.py:161
  51.4 10.2 %psum.7 = f32[768]{0:T(1024)S(1)} all-reduce(f32[768]{0:T(1024)S(1)} %reshape.7026), channel_id=1, replica_groups=mesh['ta'=8,'gz'=4] {'gz'}, use_global_device_ids=true, to_apply=%region_0.1 | all-reduce | flops 768 | bytes 6144 | tf_op jit(solution)/shard_map/psum | solution.py:164
  61.7 0.6 fusion
  62.2 0.2 dynamic-update-slice
  62.5 7.4 %all-reduce = bf16[768]{0:T(1024)(128)(2,1)S(1)} all-reduce(f32[768]{0:T(1024)S(1)} %dynamic-update-slice), channel_id=1, replica_groups=mesh['ta'=8,'gz'=4] {'gz'}, use_global_device_ids=true, to_apply=%add | all-reduce | flops 768 | bytes 4608
  70.0 0.2 convolution_convert_fusion
  70.3 1.3 %multiply_reduce_fusion = f32[4,512,2,4,3]{1,0,4,3,2:T(4,128)S(1)} fusion(f32[4,512,24]{1,0,2:T(4,128)S(1)} %bitcast_convert_fusion.1, bf16[24,2,4,3,1,4,512]{6,5,4,3,2,1,0:T(4,128)(2,1)S(1)} %copy-done.1), kind=kLoop, calls=%fused_computation | loop fusion | flops 3489792 | bytes 2752512 | tf_op jit(solution)/shard_map/vrsctzn,vtzn->rsctzn/dot_general | solution.py:174
  71.6 0.7 %bitcast_add_fusion = f32[2,4,3,1,4,512]{5,4,3,2,1,0:T(4,128)} fusion(f32[2,4,3,1,4,512]{5,4,3,2,1,0:T(4,128)S(1)} %get-tuple-element.7, f32[4,512,2,4,3]{1,0,4,3,2:T(4,128)S(1)} %multiply_reduce_fusion), kind=kLoop, calls=%fused_computation.45 | loop fusion | flops 49152 | bytes 589824 | tf_op jit(solution)/shard_map/add | solution.py:180
  (643 shorter events, 9.0 us)
Async XLA Ops:
  0.0 61.7 %copy-start = (f32[1,192,768]{2,1,0:T(8,128)S(1)}, f32[1,192,768]{2,1,0:T(8,128)}, u32[]{:S(2)}) copy-start(f32[1,192,768]{2,1,0:T(8,128)} %param.11) | copy-start | bytes 1769476
  1.9 23.1 %collective-permute-start.2 = (bf16[2,4,3,1,4,512]{5,4,2,3,1,0:T(4,128)(2,1)S(1)}, bf16[2,4,3,1,4,512]{5,4,2,3,1,0:T(4,128)(2,1)S(1)}, u32[]{:S(2)}, u32[]{:S(2)}) collective-permute-start(bf16[2,4,3,1,4,512]{5,4,2,3,1,0:T(4,128)(2,1)S(1)} %get-tuple-element.9), channel_id=1, source_target_pairs={{4,0},{8,4},{12,8},{16,12},{20,16},{24,20},{28,24},{0,28},{5,1},{9... | collective-permute-start | bytes 294920 | tf_op jit(solution)/shard_map/ppermute | solution.py:30
  7.1 15.5 %collective-permute-start = (bf16[2,4,3,1,1,512]{5,4,2,3,1,0:T(2,128)(2,1)}, bf16[2,4,3,1,1,512]{5,4,2,3,1,0:T(2,128)(2,1)}, u32[]{:S(2)}, u32[]{:S(2)}) collective-permute-start(bf16[2,4,3,1,1,512]{5,4,2,3,1,0:T(2,128)(2,1)} %slice.2542), channel_id=1, source_target_pairs={{1,0},{2,1},{3,2},{0,3},{5,4},{6,5},{7,6},{4,7},{9,8},{10,9},{11,1... | collective-permute-start | bytes 73736 | tf_op jit(solution)/shard_map/ppermute | solution.py:30
  13.1 11.0 %collective-permute-start.1 = (bf16[2,4,3,1,1,512]{5,4,2,3,1,0:T(2,128)(2,1)}, bf16[2,4,3,1,1,512]{5,4,2,3,1,0:T(2,128)(2,1)}, u32[]{:S(2)}, u32[]{:S(2)}) collective-permute-start(bf16[2,4,3,1,1,512]{5,4,2,3,1,0:T(2,128)(2,1)} %fusion.39), channel_id=1, source_target_pairs={{3,0},{0,1},{1,2},{2,3},{7,4},{4,5},{5,6},{6,7},{11,8},{8,9},{9,10... | collective-permute-start | bytes 73736 | tf_op jit(solution)/shard_map/ppermute | solution.py:30
  14.5 11.2 %collective-permute-start.3 = (bf16[2,4,3,1,4,512]{5,4,2,3,1,0:T(4,128)(2,1)S(1)}, bf16[2,4,3,1,4,512]{5,4,2,3,1,0:T(4,128)(2,1)}, u32[]{:S(2)}, u32[]{:S(2)}) collective-permute-start(bf16[2,4,3,1,4,512]{5,4,2,3,1,0:T(4,128)(2,1)S(1)} %pad_maximum_fusion.7), channel_id=1, source_target_pairs={{28,0},{0,4},{4,8},{8,12},{12,16},{16,20},{20,24},{24,28},{29,1},{... | collective-permute-start | bytes 294920 | tf_op jit(solution)/shard_map/ppermute | solution.py:30
  16.1 2.8 %copy-start.108 = (f32[4,512]{1,0:T(4,128)}, f32[4,512]{1,0:T(4,128)S(1)}, u32[]{:S(2)}) copy-start(f32[4,512]{1,0:T(4,128)S(1)} %get-tuple-element.456) | copy-start | bytes 24580
  16.1 2.8 %copy-start.110 = (f32[4,512]{1,0:T(4,128)}, f32[4,512]{1,0:T(4,128)S(1)}, u32[]{:S(2)}) copy-start(f32[4,512]{1,0:T(4,128)S(1)} %get-tuple-element.459) | copy-start | bytes 24580
  16.1 2.8 %copy-start.112 = (f32[4,512]{1,0:T(4,128)}, f32[4,512]{1,0:T(4,128)S(1)}, u32[]{:S(2)}) copy-start(f32[4,512]{1,0:T(4,128)S(1)} %get-tuple-element.462) | copy-start | bytes 24580
  16.1 2.9 %copy-start.102 = (f32[4,512]{1,0:T(4,128)}, f32[4,512]{1,0:T(4,128)S(1)}, u32[]{:S(2)}) copy-start(f32[4,512]{1,0:T(4,128)S(1)} %get-tuple-element.454) | copy-start | bytes 24580
  16.1 2.9 %copy-start.104 = (f32[4,512]{1,0:T(4,128)}, f32[4,512]{1,0:T(4,128)S(1)}, u32[]{:S(2)}) copy-start(f32[4,512]{1,0:T(4,128)S(1)} %get-tuple-element.457) | copy-start | bytes 24580
  16.2 2.9 %copy-start.106 = (f32[4,512]{1,0:T(4,128)}, f32[4,512]{1,0:T(4,128)S(1)}, u32[]{:S(2)}) copy-start(f32[4,512]{1,0:T(4,128)S(1)} %get-tuple-element.460) | copy-start | bytes 24580
  16.2 3.0 %copy-start.96 = (f32[4,512]{1,0:T(4,128)}, f32[4,512]{1,0:T(4,128)S(1)}, u32[]{:S(2)}) copy-start(f32[4,512]{1,0:T(4,128)S(1)} %get-tuple-element.455) | copy-start | bytes 24580
  16.2 3.0 %copy-start.98 = (f32[4,512]{1,0:T(4,128)}, f32[4,512]{1,0:T(4,128)S(1)}, u32[]{:S(2)}) copy-start(f32[4,512]{1,0:T(4,128)S(1)} %get-tuple-element.458) | copy-start | bytes 24580
  16.2 3.0 %copy-start.100 = (f32[4,512]{1,0:T(4,128)}, f32[4,512]{1,0:T(4,128)S(1)}, u32[]{:S(2)}) copy-start(f32[4,512]{1,0:T(4,128)S(1)} %get-tuple-element.461) | copy-start | bytes 24580
  19.5 4.3 %copy-start.54 = (f32[4,512]{1,0:T(4,128)S(1)}, f32[4,512]{1,0:T(4,128)}, u32[]{:S(2)}) copy-start(f32[4,512]{1,0:T(4,128)} %get-tuple-element.296) | copy-start | bytes 24580
  19.5 4.3 %copy-start.56 = (f32[4,512]{1,0:T(4,128)S(1)}, f32[4,512]{1,0:T(4,128)}, u32[]{:S(2)}) copy-start(f32[4,512]{1,0:T(4,128)} %get-tuple-element.303) | copy-start | bytes 24580
  19.5 4.3 %copy-start.58 = (f32[4,512]{1,0:T(4,128)S(1)}, f32[4,512]{1,0:T(4,128)}, u32[]{:S(2)}) copy-start(f32[4,512]{1,0:T(4,128)} %get-tuple-element.304) | copy-start | bytes 24580
  19.7 4.1 %copy-start.48 = (f32[4,512]{1,0:T(4,128)S(1)}, f32[4,512]{1,0:T(4,128)}, u32[]{:S(2)}) copy-start(f32[4,512]{1,0:T(4,128)} %get-tuple-element.300) | copy-start | bytes 24580
  19.7 4.1 %copy-start.50 = (f32[4,512]{1,0:T(4,128)S(1)}, f32[4,512]{1,0:T(4,128)}, u32[]{:S(2)}) copy-start(f32[4,512]{1,0:T(4,128)} %get-tuple-element.301) | copy-start | bytes 24580
  19.7 4.1 %copy-start.52 = (f32[4,512]{1,0:T(4,128)S(1)}, f32[4,512]{1,0:T(4,128)}, u32[]{:S(2)}) copy-start(f32[4,512]{1,0:T(4,128)} %get-tuple-element.302) | copy-start | bytes 24580
  19.8 4.1 %copy-start.42 = (f32[4,512]{1,0:T(4,128)S(1)}, f32[4,512]{1,0:T(4,128)}, u32[]{:S(2)}) copy-start(f32[4,512]{1,0:T(4,128)} %get-tuple-element.297) | copy-start | bytes 24580
  19.8 4.1 %copy-start.44 = (f32[4,512]{1,0:T(4,128)S(1)}, f32[4,512]{1,0:T(4,128)}, u32[]{:S(2)}) copy-start(f32[4,512]{1,0:T(4,128)} %get-tuple-element.298) | copy-start | bytes 24580
  19.8 4.1 %copy-start.46 = (f32[4,512]{1,0:T(4,128)S(1)}, f32[4,512]{1,0:T(4,128)}, u32[]{:S(2)}) copy-start(f32[4,512]{1,0:T(4,128)} %get-tuple-element.299) | copy-start | bytes 24580
  20.5 4.8 %copy-start.36 = (f32[4,512]{1,0:T(4,128)S(1)}, f32[4,512]{1,0:T(4,128)}, u32[]{:S(2)}) copy-start(f32[4,512]{1,0:T(4,128)} %get-tuple-element.323) | copy-start | bytes 24580
  20.5 4.8 %copy-start.38 = (f32[4,512]{1,0:T(4,128)S(1)}, f32[4,512]{1,0:T(4,128)}, u32[]{:S(2)}) copy-start(f32[4,512]{1,0:T(4,128)} %get-tuple-element.330) | copy-start | bytes 24580
  20.5 4.8 %copy-start.40 = (f32[4,512]{1,0:T(4,128)S(1)}, f32[4,512]{1,0:T(4,128)}, u32[]{:S(2)}) copy-start(f32[4,512]{1,0:T(4,128)} %get-tuple-element.331) | copy-start | bytes 24580
  20.6 4.8 %copy-start.30 = (f32[4,512]{1,0:T(4,128)S(1)}, f32[4,512]{1,0:T(4,128)}, u32[]{:S(2)}) copy-start(f32[4,512]{1,0:T(4,128)} %get-tuple-element.327) | copy-start | bytes 24580
  20.6 4.8 %copy-start.32 = (f32[4,512]{1,0:T(4,128)S(1)}, f32[4,512]{1,0:T(4,128)}, u32[]{:S(2)}) copy-start(f32[4,512]{1,0:T(4,128)} %get-tuple-element.328) | copy-start | bytes 24580
  20.6 4.8 %copy-start.34 = (f32[4,512]{1,0:T(4,128)S(1)}, f32[4,512]{1,0:T(4,128)}, u32[]{:S(2)}) copy-start(f32[4,512]{1,0:T(4,128)} %get-tuple-element.329) | copy-start | bytes 24580
  20.6 4.7 %copy-start.24 = (f32[4,512]{1,0:T(4,128)S(1)}, f32[4,512]{1,0:T(4,128)}, u32[]{:S(2)}) copy-start(f32[4,512]{1,0:T(4,128)} %get-tuple-element.324) | copy-start | bytes 24580
  20.7 4.7 %copy-start.26 = (f32[4,512]{1,0:T(4,128)S(1)}, f32[4,512]{1,0:T(4,128)}, u32[]{:S(2)}) copy-start(f32[4,512]{1,0:T(4,128)} %get-tuple-element.325) | copy-start | bytes 24580
  20.7 4.7 %copy-start.28 = (f32[4,512]{1,0:T(4,128)S(1)}, f32[4,512]{1,0:T(4,128)}, u32[]{:S(2)}) copy-start(f32[4,512]{1,0:T(4,128)} %get-tuple-element.326) | copy-start | bytes 24580
  31.2 5.0 %copy-start.73 = (f32[4,512]{1,0:T(4,128)S(1)}, f32[4,512]{1,0:T(4,128)}, u32[]{:S(2)}) copy-start(f32[4,512]{1,0:T(4,128)} %copy-done.72) | copy-start | bytes 24580
  31.2 5.0 %copy-start.75 = (f32[4,512]{1,0:T(4,128)S(1)}, f32[4,512]{1,0:T(4,128)}, u32[]{:S(2)}) copy-start(f32[4,512]{1,0:T(4,128)} %copy-done.74) | copy-start | bytes 24580
  31.2 5.0 %copy-start.77 = (f32[4,512]{1,0:T(4,128)S(1)}, f32[4,512]{1,0:T(4,128)}, u32[]{:S(2)}) copy-start(f32[4,512]{1,0:T(4,128)} %copy-done.76) | copy-start | bytes 24580
  31.3 5.0 %copy-start.67 = (f32[4,512]{1,0:T(4,128)S(1)}, f32[4,512]{1,0:T(4,128)}, u32[]{:S(2)}) copy-start(f32[4,512]{1,0:T(4,128)} %copy-done.66) | copy-start | bytes 24580
  31.3 5.0 %copy-start.69 = (f32[4,512]{1,0:T(4,128)S(1)}, f32[4,512]{1,0:T(4,128)}, u32[]{:S(2)}) copy-start(f32[4,512]{1,0:T(4,128)} %copy-done.68) | copy-start | bytes 24580
  31.3 5.0 %copy-start.71 = (f32[4,512]{1,0:T(4,128)S(1)}, f32[4,512]{1,0:T(4,128)}, u32[]{:S(2)}) copy-start(f32[4,512]{1,0:T(4,128)} %copy-done.70) | copy-start | bytes 24580
  31.4 4.9 %copy-start.61 = (f32[4,512]{1,0:T(4,128)S(1)}, f32[4,512]{1,0:T(4,128)}, u32[]{:S(2)}) copy-start(f32[4,512]{1,0:T(4,128)} %copy-done.60) | copy-start | bytes 24580
  31.4 4.9 %copy-start.63 = (f32[4,512]{1,0:T(4,128)S(1)}, f32[4,512]{1,0:T(4,128)}, u32[]{:S(2)}) copy-start(f32[4,512]{1,0:T(4,128)} %copy-done.62) | copy-start | bytes 24580
  31.5 4.9 %copy-start.65 = (f32[4,512]{1,0:T(4,128)S(1)}, f32[4,512]{1,0:T(4,128)}, u32[]{:S(2)}) copy-start(f32[4,512]{1,0:T(4,128)} %copy-done.64) | copy-start | bytes 24580
  32.6 12.5 %collective-permute-start.6 = (bf16[2,4,3,1,4,512]{5,4,3,2,1,0:T(4,128)(2,1)S(1)}, bf16[2,4,3,1,4,512]{5,4,3,2,1,0:T(4,128)(2,1)S(1)}, u32[]{:S(2)}, u32[]{:S(2)}) collective-permute-start(bf16[2,4,3,1,4,512]{5,4,3,2,1,0:T(4,128)(2,1)S(1)} %get-tuple-element.6), channel_id=1, source_target_pairs={{4,0},{8,4},{12,8},{16,12},{20,16},{24,20},{28,24},{0,28},{5,1},{9... | collective-permute-start | bytes 294920 | tf_op jit(solution)/shard_map/ppermute | solution.py:30
  36.5 5.2 %copy-start.55 = (f32[4,512]{1,0:T(4,128)S(1)}, f32[4,512]{1,0:T(4,128)}, u32[]{:S(2)}) copy-start(f32[4,512]{1,0:T(4,128)} %get-tuple-element.296) | copy-start | bytes 24580
  36.5 5.2 %copy-start.57 = (f32[4,512]{1,0:T(4,128)S(1)}, f32[4,512]{1,0:T(4,128)}, u32[]{:S(2)}) copy-start(f32[4,512]{1,0:T(4,128)} %get-tuple-element.303) | copy-start | bytes 24580
  36.5 5.2 %copy-start.59 = (f32[4,512]{1,0:T(4,128)S(1)}, f32[4,512]{1,0:T(4,128)}, u32[]{:S(2)}) copy-start(f32[4,512]{1,0:T(4,128)} %get-tuple-element.304) | copy-start | bytes 24580
  36.5 5.2 %copy-start.49 = (f32[4,512]{1,0:T(4,128)S(1)}, f32[4,512]{1,0:T(4,128)}, u32[]{:S(2)}) copy-start(f32[4,512]{1,0:T(4,128)} %get-tuple-element.300) | copy-start | bytes 24580
  36.5 5.2 %copy-start.51 = (f32[4,512]{1,0:T(4,128)S(1)}, f32[4,512]{1,0:T(4,128)}, u32[]{:S(2)}) copy-start(f32[4,512]{1,0:T(4,128)} %get-tuple-element.301) | copy-start | bytes 24580
  36.5 5.2 %copy-start.53 = (f32[4,512]{1,0:T(4,128)S(1)}, f32[4,512]{1,0:T(4,128)}, u32[]{:S(2)}) copy-start(f32[4,512]{1,0:T(4,128)} %get-tuple-element.302) | copy-start | bytes 24580
  36.6 5.2 %copy-start.43 = (f32[4,512]{1,0:T(4,128)S(1)}, f32[4,512]{1,0:T(4,128)}, u32[]{:S(2)}) copy-start(f32[4,512]{1,0:T(4,128)} %get-tuple-element.297) | copy-start | bytes 24580
  36.6 5.2 %copy-start.45 = (f32[4,512]{1,0:T(4,128)S(1)}, f32[4,512]{1,0:T(4,128)}, u32[]{:S(2)}) copy-start(f32[4,512]{1,0:T(4,128)} %get-tuple-element.298) | copy-start | bytes 24580
  36.6 5.2 %copy-start.47 = (f32[4,512]{1,0:T(4,128)S(1)}, f32[4,512]{1,0:T(4,128)}, u32[]{:S(2)}) copy-start(f32[4,512]{1,0:T(4,128)} %get-tuple-element.299) | copy-start | bytes 24580
  36.7 4.7 %collective-permute-start.4 = (bf16[2,4,3,1,1,512]{5,4,2,3,1,0:T(2,128)(2,1)S(1)}, bf16[2,4,3,1,1,512]{5,4,2,3,1,0:T(2,128)(2,1)S(1)}, u32[]{:S(2)}, u32[]{:S(2)}) collective-permute-start(bf16[2,4,3,1,1,512]{5,4,2,3,1,0:T(2,128)(2,1)S(1)} %slice.2726), channel_id=1, source_target_pairs={{1,0},{2,1},{3,2},{0,3},{5,4},{6,5},{7,6},{4,7},{9,8},{10,9},{11,1... | collective-permute-start | bytes 73736 | tf_op jit(solution)/shard_map/ppermute | solution.py:30
  39.8 5.0 %collective-permute-start.5 = (bf16[2,4,3,1,1,512]{5,4,2,1,3,0:T(2,128)(2,1)S(1)}, bf16[2,4,3,1,1,512]{5,4,2,1,3,0:T(2,128)(2,1)S(1)}, u32[]{:S(2)}, u32[]{:S(2)}) collective-permute-start(bf16[2,4,3,1,1,512]{5,4,2,1,3,0:T(2,128)(2,1)S(1)} %fusion.38), channel_id=1, source_target_pairs={{3,0},{0,1},{1,2},{2,3},{7,4},{4,5},{5,6},{6,7},{11,8},{8,9},{9,10... | collective-permute-start | bytes 73736 | tf_op jit(solution)/shard_map/ppermute | solution.py:30
  40.3 6.1 %collective-permute-start.7 = (bf16[2,4,3,1,4,512]{5,4,2,1,3,0:T(4,128)(2,1)S(1)}, bf16[2,4,3,1,4,512]{5,4,2,1,3,0:T(4,128)(2,1)S(1)}, u32[]{:S(2)}, u32[]{:S(2)}) collective-permute-start(bf16[2,4,3,1,4,512]{5,4,2,1,3,0:T(4,128)(2,1)S(1)} %pad_maximum_fusion.11), channel_id=1, source_target_pairs={{28,0},{0,4},{4,8},{8,12},{12,16},{16,20},{20,24},{24,28},{29,1},{... | collective-permute-start | bytes 294920 | tf_op jit(solution)/shard_map/ppermute | solution.py:30
  40.8 4.5 %copy-start.37 = (f32[4,512]{1,0:T(4,128)S(1)}, f32[4,512]{1,0:T(4,128)}, u32[]{:S(2)}) copy-start(f32[4,512]{1,0:T(4,128)} %get-tuple-element.323) | copy-start | bytes 24580
  40.8 4.5 %copy-start.39 = (f32[4,512]{1,0:T(4,128)S(1)}, f32[4,512]{1,0:T(4,128)}, u32[]{:S(2)}) copy-start(f32[4,512]{1,0:T(4,128)} %get-tuple-element.330) | copy-start | bytes 24580
  40.9 4.5 %copy-start.41 = (f32[4,512]{1,0:T(4,128)S(1)}, f32[4,512]{1,0:T(4,128)}, u32[]{:S(2)}) copy-start(f32[4,512]{1,0:T(4,128)} %get-tuple-element.331) | copy-start | bytes 24580
  40.9 4.6 %copy-start.31 = (f32[4,512]{1,0:T(4,128)S(1)}, f32[4,512]{1,0:T(4,128)}, u32[]{:S(2)}) copy-start(f32[4,512]{1,0:T(4,128)} %get-tuple-element.327) | copy-start | bytes 24580
  40.9 4.6 %copy-start.33 = (f32[4,512]{1,0:T(4,128)S(1)}, f32[4,512]{1,0:T(4,128)}, u32[]{:S(2)}) copy-start(f32[4,512]{1,0:T(4,128)} %get-tuple-element.328) | copy-start | bytes 24580
  40.9 4.6 %copy-start.35 = (f32[4,512]{1,0:T(4,128)S(1)}, f32[4,512]{1,0:T(4,128)}, u32[]{:S(2)}) copy-start(f32[4,512]{1,0:T(4,128)} %get-tuple-element.329) | copy-start | bytes 24580
  41.5 4.0 %copy-start.25 = (f32[4,512]{1,0:T(4,128)S(1)}, f32[4,512]{1,0:T(4,128)}, u32[]{:S(2)}) copy-start(f32[4,512]{1,0:T(4,128)} %get-tuple-element.324) | copy-start | bytes 24580
  41.5 4.0 %copy-start.27 = (f32[4,512]{1,0:T(4,128)S(1)}, f32[4,512]{1,0:T(4,128)}, u32[]{:S(2)}) copy-start(f32[4,512]{1,0:T(4,128)} %get-tuple-element.325) | copy-start | bytes 24580
  41.5 4.0 %copy-start.29 = (f32[4,512]{1,0:T(4,128)S(1)}, f32[4,512]{1,0:T(4,128)}, u32[]{:S(2)}) copy-start(f32[4,512]{1,0:T(4,128)} %get-tuple-element.326) | copy-start | bytes 24580
  47.0 2.6 %copy-start.23 = (s32[1,4,4,128]{3,1,2,0:T(4,128)S(1)}, s32[1,4,4,128]{3,1,2,0:T(4,128)}, u32[]{:S(2)}) copy-start(s32[1,4,4,128]{3,1,2,0:T(4,128)} %copy.342) | copy-start | bytes 24580
  (114 other events, 171.0 us)
where the time goes:
time: 72.8 us; the launch traced here: 72.3 us
  other arithmetic  17.7 us (24%)
  blocking collectives  17.7 us (24%)
  starting transfers between devices  13.9 us (19%)
  local copies, waits for them, and re-layouts  11.1 us (15%)
  between operations  5.53 us (8%)
  waiting for transfers between devices  4.02 us (6%)
  matrix products  2.47 us (3%)
    ppermute x8, starting transfers between devices, shifted(): return lax.ppermute(block, axis, route)  13.9 us
    psum x1, blocking collectives, shards(): coarse_resid = lax.psum(partial_sum.reshape(-1), 'gz')  10.2 us
    unnamed x1, blocking collectives  7.45 us
    ppermute x8, waiting for transfers between devices, shifted(): return lax.ppermute(block, axis, route)  4.02 us
    unnamed x344, local copies, waits for them, and re-layouts  3.28 us
    another operation x38, other arithmetic, expand(): return jnp.stack([jnp.stack(rows_re), jnp.stack(rows_im)])  1.99 us
    dot_general x1, matrix products, shards(): jnp.einsum('am,vm->av', member.astype(jnp.float32), projected.reshape(vec...  1.71 us
    unnamed x3, other arithmetic  1.58 us
  transfers between devices with their start and end apart: 8, of which 3 were waited for; matrix products, arithmetic and copies ran while one was open for 20% of the time, Pallas kernels for 0%

commit v1 on v0

v1 whole, which is shorter than its diff:
```python
import functools

import jax
import jax.numpy as jnp
from jax import lax
from jax.experimental import pallas as pl
from jax.experimental.pallas import tpu as pltpu
from jax.sharding import PartitionSpec as P

LX = 32
NAGG = 32
NV = 24
NCOMP = 24
HALF = 256
GROUPS = 8

MESH = pl.DeviceIdType.MESH
F32 = jnp.float32
BF16 = jnp.bfloat16

spin_perms = ((3, 2, 1, 0), (3, 2, 1, 0), (2, 3, 0, 1), (2, 3, 0, 1))
spin_coefs = (
    ((1, -1), (1, -1), (1, 1), (1, 1)),
    ((0, -1), (0, 1), (0, 1), (0, -1)),
    ((1, -1), (1, 1), (1, 1), (1, -1)),
    ((0, 1), (0, 1), (0, 1), (0, 1)),
)


def add_signed(base, sign, value):
    return base + value if sign > 0 else base - value


def phase_terms(coef, sign):
    imag, coef_sign = coef
    total_sign = coef_sign * sign
    if imag:
        return (1, -total_sign), (0, total_sign)
    return (0, total_sign), (1, total_sign)


def project(field, direction, sign):
    parts = [[None, None], [None, None]]
    for slot in range(2):
        other = spin_perms[direction][slot]
        terms = phase_terms(spin_coefs[direction][slot], sign)
        for part in range(2):
            from_part, term_sign = terms[part]
            parts[part][slot] = add_signed(
                field[pl.ds(part * 12 + slot * 3, 3)],
                term_sign,
                field[pl.ds(from_part * 12 + other * 3, 3)],
            )
    return parts


def accumulate(total, half, direction, sign):
    for slot in range(2):
        other = spin_perms[direction][slot]
        terms = phase_terms(spin_coefs[direction][other], sign)
        for part in range(2):
            at = pl.ds(part * 12 + slot * 3, 3)
            total[at] = total[at] + half[part][slot]
            from_part, term_sign = terms[part]
            at = pl.ds(part * 12 + other * 3, 3)
            total[at] = add_signed(total[at], term_sign, half[from_part][slot])


def mix(links, direction, half, dagger):
    out = [[None, None], [None, None]]
    for slot in range(2):
        acc_re = acc_im = None
        for col in range(3):
            if dagger:
                link_re = links[direction, 0, col]
                link_im = links[direction, 1, col]
            else:
                link_re = links[direction, 0, :, col]
                link_im = links[direction, 1, :, col]
            re = half[0][slot][col][None]
            im = half[1][slot][col][None]
            if dagger:
                part_re = link_re * re + link_im * im
                part_im = link_re * im - link_im * re
            else:
                part_re = link_re * re - link_im * im
                part_im = link_re * im + link_im * re
            acc_re = part_re if acc_re is None else acc_re + part_re
            acc_im = part_im if acc_im is None else acc_im + part_im
        out[0][slot] = acc_re
        out[1][slot] = acc_im
    return out


def per_part(fn, half):
    return [[fn(half[part][slot]) for slot in range(2)] for part in range(2)]


def stack_half(half):
    return jnp.concatenate([half[p][s] for p in range(2) for s in range(2)], axis=0)


def split_half(stacked):
    return [[stacked[p * 6 + s * 3 : p * 6 + s * 3 + 3] for s in range(2)] for p in range(2)]


def split_bf16(value, pieces):
    out = []
    for _ in range(pieces):
        piece = value.astype(BF16)
        out.append(piece)
        value = value - piece.astype(F32)
    return out


def kernel(
    n_ta,
    n_gz,
    rows,
    source_hbm,
    links_hbm,
    clover_hbm,
    map_hbm,
    prolong_hbm,
    inverse_hbm,
    out_ref,
    source_in,
    links_in,
    clover_in,
    map_in,
    prolong_in,
    inverse,
    source,
    links,
    diag,
    recip,
    prolong,
    field,
    total,
    member,
    expander,
    projected,
    t_send,
    t_recv,
    z_send,
    z_recv,
    r_send,
    r_recv,
    c_send,
    c_recv,
    in_sem,
    halo_send_sem,
    halo_recv_sem,
    r_send_sem,
    r_recv_sem,
    c_send_sem,
    c_recv_sem,
):
    loads = [
        pltpu.make_async_copy(src, dst, in_sem.at[i])
        for i, (src, dst) in enumerate(
            (
                (source_hbm, source_in),
                (clover_hbm, clover_in),
                (links_hbm, links_in),
                (map_hbm, map_in),
                (prolong_hbm, prolong_in),
                (inverse_hbm, inverse),
            )
        )
    ]
    for load in loads:
        load.start()
    load_source, load_clover, load_links, load_map, load_prolong, load_inverse = loads

    ta = lax.axis_index("ta")
    gz = lax.axis_index("gz")
    t_before = lax.rem(ta + n_ta - 1, n_ta)
    t_after = lax.rem(ta + 1, n_ta)
    z_before = lax.rem(gz + n_gz - 1, n_gz)
    z_after = lax.rem(gz + 1, n_gz)
    peers = [lax.rem(gz + k, n_gz) for k in range(1, n_gz)]

    barrier = pltpu.get_barrier_semaphore()
    for there in (t_before, t_after):
        pl.semaphore_signal(barrier, inc=1, device_id=(there, gz), device_id_type=MESH)
    for there in peers:
        pl.semaphore_signal(barrier, inc=1, device_id=(ta, there), device_id_type=MESH)

    sub = lax.broadcasted_iota(jnp.int32, (8, HALF), 0)
    lane = lax.broadcasted_iota(jnp.int32, (8, HALF), 1)
    z_at = jnp.bitwise_and(sub, 3)
    x_at = jnp.bitwise_and(lane, LX - 1)

    def widen(dst, src, at, size):
        block = src[pl.ds(at, size)].astype(F32)
        dst[pl.ds(at, size), 0:4, :] = block[:, :, :HALF]
        dst[pl.ds(at, size), 4:8, :] = block[:, :, HALF:]

    load_source.wait()
    widen(source, source_in, 0, NCOMP)
    load_clover.wait()
    widen(diag, clover_in, 0, 12)
    for at in range(0, 12, 3):
        here = pl.ds(at, 3)
        wide = diag[here] + 3.6
        diag[here] = wide
        inv = 1.0 / wide
        recip[here] = inv
        for part in range(2):
            there = pl.ds(part * 12 + at, 3)
            field[there] = source[there] * inv

    pl.semaphore_wait(barrier, 2 + n_gz - 1)

    def select(mask, first, second):
        return jnp.where(mask[None], first, second)

    def shift(direction, step):
        def x_shift(value):
            if step > 0:
                return select(
                    x_at == LX - 1, pltpu.roll(value, LX - 1, 2), pltpu.roll(value, HALF - 1, 2)
                )
            return select(x_at == 0, pltpu.roll(value, HALF - LX + 1, 2), pltpu.roll(value, 1, 2))

        def y_shift(value):
            rolled = pltpu.roll(value, HALF - LX if step > 0 else LX, 2)
            swapped = pltpu.roll(rolled, 4, 1)
            return select(lane >= HALF - LX if step > 0 else lane < LX, swapped, rolled)

        return x_shift if direction == 0 else y_shift

    def pack_rows(stacked, row):
        blocks = []
        for block in range(3):
            packed = None
            for j in range(4):
                value = stacked[block * 4 + j]
                turn = (j - row) % 8
                if turn:
                    value = pltpu.roll(value, turn, 0)
                packed = value if packed is None else jnp.where(z_at == j, value, packed)
            blocks.append(packed)
        blocks.append(jnp.zeros((8, HALF), F32))
        return jnp.concatenate(blocks, axis=0).astype(BF16)

    def fill_rows(stacked, packed, row, turn):
        out = []
        for j in range(12):
            halo = packed[j // 4]
            by = (row - j % 4) % 8
            if by:
                halo = pltpu.roll(halo, by, 0)
            out.append(jnp.where(z_at == row, halo, pltpu.roll(stacked[j], turn, 0))[None])
        return jnp.concatenate(out, axis=0)

    def halo_copy(sweep, which, src, dst, device):
        return pltpu.make_async_remote_copy(
            src_ref=src,
            dst_ref=dst,
            send_sem=halo_send_sem.at[sweep, which],
            recv_sem=halo_recv_sem.at[sweep, which],
            device_id=device,
            device_id_type=MESH,
        )

    def hopping(sweep, before_links, beside):
        copies = [
            halo_copy(sweep, 0, t_send.at[sweep, 0], t_recv.at[sweep, 0], (t_before, gz)),
            halo_copy(sweep, 1, t_send.at[sweep, 1], t_recv.at[sweep, 1], (t_after, gz)),
            halo_copy(sweep, 2, z_send.at[sweep, 0], z_recv.at[sweep, 0], (ta, z_before)),
            halo_copy(sweep, 3, z_send.at[sweep, 1], z_recv.at[sweep, 1], (ta, z_after)),
        ]
        fwd_t = stack_half(project(field, 3, -1))
        t_send[sweep, 0] = fwd_t.reshape(96, HALF).astype(BF16)
        copies[0].start()
        fwd_z = stack_half(project(field, 2, -1))
        z_send[sweep, 0] = pack_rows(fwd_z, 0)
        copies[2].start()
        before_links()
        back_t = stack_half(mix(links, 3, project(field, 3, 1), True))
        t_send[sweep, 1] = back_t.reshape(96, HALF).astype(BF16)
        copies[1].start()
        back_z = stack_half(mix(links, 2, project(field, 2, 1), True))
        z_send[sweep, 1] = pack_rows(back_z, 3)
        copies[3].start()

        total[...] = jnp.zeros((NCOMP, 8, HALF), F32)
        for direction in range(2):
            ahead = per_part(shift(direction, 1), project(field, direction, -1))
            accumulate(total, mix(links, direction, ahead, False), direction, -1)
            behind = per_part(
                shift(direction, -1), mix(links, direction, project(field, direction, 1), True)
            )
            accumulate(total, behind, direction, 1)
        beside()
        for copy in copies:
            copy.wait()
        ahead_z = fill_rows(
            stack_half(project(field, 2, -1)),
            z_recv[sweep, 0].astype(F32).reshape(4, 8, HALF),
            3,
            7,
        )
        accumulate(total, mix(links, 2, split_half(ahead_z), False), 2, -1)
        behind_z = fill_rows(back_z, z_recv[sweep, 1].astype(F32).reshape(4, 8, HALF), 0, 1)
        accumulate(total, split_half(behind_z), 2, 1)
        ahead_t = t_recv[sweep, 0].astype(F32).reshape(12, 8, HALF)
        accumulate(total, mix(links, 3, split_half(ahead_t), False), 3, -1)
        behind_t = t_recv[sweep, 1].astype(F32).reshape(12, 8, HALF)
        accumulate(total, split_half(behind_t), 3, 1)

    def widen_links():
        load_links.wait()
        for direction in (3, 2, 1, 0):
            for part in range(2):
                for row in range(3):
                    at = direction * 18 + part * 9 + row * 3
                    block = links_in[pl.ds(at, 3)].astype(F32)
                    links[direction, part, row, :, 0:4, :] = block[:, :, :HALF]
                    links[direction, part, row, :, 4:8, :] = block[:, :, HALF:]

    def widen_prolong(start, stop):
        def step(i, carry):
            widen(prolong, prolong_in, i * 12, 12)
            return carry

        lax.fori_loop(start, stop, step, 0)

    def beside_first():
        load_map.wait()
        labels = lax.broadcasted_iota(jnp.int32, (NAGG, HALF), 0)
        ones = []
        for half in range(2):
            for z in range(4):
                row = map_in[pl.ds(z, 1), pl.ds(half * HALF, HALF)]
                ones.append((labels == row).astype(F32))
        member[...] = jnp.concatenate(ones, axis=0).astype(BF16)
        low = jnp.bitwise_and(
            lax.broadcasted_iota(jnp.int32, (HALF, NV * NAGG), 0), NAGG - 1
        ) * NV
        column = lax.broadcasted_iota(jnp.int32, (HALF, NV * NAGG), 1)
        inside = jnp.logical_and(column >= low, column < low + NV)
        expander[...] = inside.astype(F32).astype(BF16)
        load_prolong.wait()
        widen_prolong(0, 24)

    hopping(0, widen_links, beside_first)
    for at in range(0, 24, 3):
        here = pl.ds(at, 3)
        scale = pl.ds(at % 12, 3)
        first = field[here]
        resid = source[here] - diag[scale] * first + 0.5 * total[here]
        field[here] = first + resid * recip[scale]
    hopping(1, lambda: None, lambda: widen_prolong(24, 48))
    for at in range(0, 24, 3):
        here = pl.ds(at, 3)
        second = field[here]
        total[here] = source[here] - diag[pl.ds(at % 12, 3)] * second + 0.5 * total[here]

    def restrict(i, carry):
        accs = [None] * 4
        for comp in range(NCOMP):
            resid = total[comp]
            for k in range(4):
                term = prolong[(i * 4 + k) * NCOMP + comp] * resid
                accs[k] = term if accs[k] is None else accs[k] + term
        for k in range(4):
            projected[pl.ds((i * 4 + k) * 8, 8)] = accs[k]
        return carry

    lax.fori_loop(0, NV // 4, restrict, 0)

    member_value = member[...]
    sums = None
    for piece in split_bf16(projected[...], 3):
        term = lax.dot_general(
            piece, member_value, (((1,), (1,)), ((), ())), preferred_element_type=F32
        )
        sums = term if sums is None else sums + term
    own_group = (jnp.right_shift(lane, 5) == sub)[None]
    sums = jnp.sum(jnp.where(own_group, sums.reshape(NV, 8, HALF), 0.0), axis=1)
    spread_out = None
    expander_value = expander[...]
    for piece in split_bf16(sums, 3):
        term = jnp.dot(piece, expander_value, preferred_element_type=F32)
        spread_out = term if spread_out is None else spread_out + term
    column = lax.broadcasted_iota(jnp.int32, (NV, NV * NAGG), 1)
    vector = column - NV * jnp.right_shift(column * 2731, 16)
    at_vector = lax.broadcasted_iota(jnp.int32, (NV, NV * NAGG), 0) == vector
    r_send[...] = jnp.sum(jnp.where(at_vector, spread_out, 0.0), axis=0, keepdims=True)

    def to_peers(src, dst, send_sem, recv_sem):
        copies = [
            pltpu.make_async_remote_copy(
                src_ref=src,
                dst_ref=dst.at[k],
                send_sem=send_sem.at[k],
                recv_sem=recv_sem.at[k],
                device_id=(ta, there),
                device_id_type=MESH,
            )
            for k, there in enumerate(peers)
        ]
        for copy in copies:
            copy.start()
        return copies

    copies = to_peers(r_send, r_recv, r_send_sem, r_recv_sem)
    load_inverse.wait()
    for copy in copies:
        copy.wait()
    coarse = r_send[...]
    for k in range(n_gz - 1):
        coarse = coarse + r_recv[k]
    own_rows = jnp.sum(inverse[...] * coarse, axis=1, keepdims=True)
    label = jnp.bitwise_and(lax.broadcasted_iota(jnp.int32, (NV, 128), 1), NAGG - 1)
    owned = rows // NV
    placed = jnp.zeros((NV, 128), F32)
    for k in range(owned):
        placed = jnp.where(label == gz * owned + k, own_rows[k * NV : (k + 1) * NV], placed)
    c_send[...] = placed
    copies = to_peers(c_send, c_recv, c_send_sem, c_recv_sem)
    for copy in copies:
        copy.wait()
    correction = c_send[...]
    for k in range(n_gz - 1):
        correction = correction + c_recv[k]
    correction = jnp.concatenate([correction, correction], axis=1)
    lhs = jnp.where(own_group, jnp.broadcast_to(correction[:, None], (NV, 8, HALF)), 0.0)
    projected[...] = jnp.dot(
        lhs.reshape(NV * 8, HALF).astype(BF16), member_value, preferred_element_type=F32
    )

    def smooth(i, carry):
        accs = [field[i * 4 + k] for k in range(4)]
        for v in range(NV):
            weight = projected[pl.ds(v * 8, 8)]
            for k in range(4):
                accs[k] = accs[k] + prolong[v * NCOMP + i * 4 + k] * weight
        for k in range(4):
            out_ref[i * 4 + k, :, 0:HALF] = accs[k][0:4]
            out_ref[i * 4 + k, :, HALF : 2 * HALF] = accs[k][4:8]
        return carry

    lax.fori_loop(0, NCOMP // 4, smooth, 0)


def shards(n_ta, n_gz, source, links, clover, agg_map, prolong, inverse):
    rows = inverse.shape[1]
    vmem = pltpu.VMEM
    dma = pltpu.SemaphoreType.DMA
    out = pl.pallas_call(
        functools.partial(kernel, n_ta, n_gz, rows),
        out_shape=jax.ShapeDtypeStruct((24, 4, 512), F32),
        in_specs=[pl.BlockSpec(memory_space=pl.ANY)] * 6,
        out_specs=pl.BlockSpec(memory_space=pltpu.VMEM),
        scratch_shapes=[
            vmem((24, 4, 512), BF16),
            vmem((72, 4, 512), BF16),
            vmem((12, 4, 512), F32),
            vmem((4, 512), jnp.int32),
            vmem((576, 4, 512), BF16),
            vmem((rows, 768), F32),
            vmem((24, 8, HALF), F32),
            vmem((4, 2, 3, 3, 8, HALF), F32),
            vmem((12, 8, HALF), F32),
            vmem((12, 8, HALF), F32),
            vmem((576, 8, HALF), F32),
            vmem((24, 8, HALF), F32),
            vmem((24, 8, HALF), F32),
            vmem((256, HALF), BF16),
            vmem((256, 768), BF16),
            vmem((192, HALF), F32),
            vmem((2, 2, 96, HALF), BF16),
            vmem((2, 2, 96, HALF), BF16),
            vmem((2, 2, 32, HALF), BF16),
            vmem((2, 2, 32, HALF), BF16),
            vmem((1, 768), F32),
            vmem((n_gz - 1, 1, 768), F32),
            vmem((NV, 128), F32),
            vmem((n_gz - 1, NV, 128), F32),
            dma((6,)),
            dma((2, 4)),
            dma((2, 4)),
            dma((n_gz - 1,)),
            dma((n_gz - 1,)),
            dma((n_gz - 1,)),
            dma((n_gz - 1,)),
        ],
        compiler_params=pltpu.CompilerParams(
            collective_id=0, has_side_effects=True, vmem_limit_bytes=32 * 1024 * 1024
        ),
        cost_estimate=pl.CostEstimate(flops=20000000, bytes_accessed=4000000, transcendentals=0),
    )(
        source.reshape(24, 4, 512),
        links.reshape(72, 4, 512),
        clover.reshape(12, 4, 512),
        agg_map.reshape(4, 512),
        prolong.reshape(576, 4, 512),
        inverse.reshape(rows, 768),
    )
    return out.reshape(2, 4, 3, 1, 4, 512)


def solution(mesh):
    return jax.shard_map(
        functools.partial(shards, mesh.shape["ta"], mesh.shape["gz"]),
        mesh=mesh,
        in_specs=(
            P(None, None, None, "ta", "gz", None),
            P(None, None, None, None, "ta", "gz", None),
            P(None, None, "ta", "gz", None),
            P("ta", "gz", None),
            P(None, None, None, None, "ta", "gz", None),
            P("ta", "gz", None),
        ),
        out_specs=P(None, None, None, "ta", "gz", None),
        check_vma=False,
    )
```

time: 72.8 us -> 29.1 us (0.40)
  Pallas kernels: 0 us -> 21.9 us
  other arithmetic: 17.7 us -> 0 us
  blocking collectives: 17.7 us -> 0 us
  starting transfers between devices: 13.9 us -> 0 us
  between operations: 5.53 us -> 0.02 us
  local copies, waits for them, and re-layouts: 11.1 us -> 6.85 us
  waiting for transfers between devices: 4.02 us -> 0 us
  matrix products: 2.47 us -> 0 us
    pallas_call x0 -> x1, Pallas kernels: none -> 21.9 us  [shards(): pl.pallas_call(functools.partial(kernel, n_ta, n_gz, rows), out_shape=jax...]
    ppermute x8 -> x0, starting transfers between devices: 13.9 us -> none  [shifted(): return lax.ppermute(block, axis, route)]
    psum x1 -> x0, blocking collectives: 10.2 us -> none  [shards(): coarse_resid = lax.psum(partial_sum.reshape(-1), 'gz')]
    unnamed x1 -> x0, blocking collectives: 7.45 us -> none
    convert_element_type x28 -> x0, other arithmetic: 5.95 us -> none  [the longest x2 1.29 us: hopping(): wide = spinor.astype(jnp.float32)]
    another operation x123 -> x0, other arithmetic: 4.15 us -> none  [the longest x38 1.99 us: expand(): return jnp.stack([jnp.stack(rows_re), jnp.stack(rows_im)])]
    ppermute x8 -> x0, waiting for transfers between devices: 4.02 us -> none  [shifted(): return lax.ppermute(block, axis, route)]
    unnamed x344 -> x13, local copies, waits for them, and re-layouts: 3.28 us -> 6.85 us
  transfers between devices with their start and end apart: 8 -> 0, of which waited for: 3 -> 0; matrix products, arithmetic and copies ran while one was open for 20% -> 0% of each run, Pallas kernels for 0% -> 0%
where the time goes in v1:
time: 29.1 us; the launch traced here: 28.8 us
  Pallas kernels  21.9 us (75%)
  local copies, waits for them, and re-layouts  6.85 us (24%)
    pallas_call x1, Pallas kernels, shards(): pl.pallas_call(functools.partial(kernel, n_ta, n_gz, rows), out_shape=jax...  21.9 us
    unnamed x13, local copies, waits for them, and re-layouts  6.85 us

profile of v1, /device:TPU:0, one launch (start us, length us, event | category | flops | bytes accessed | tf_op | source)
XLA Modules:
  0.0 28.8 jit_solution(16469658093250266494)
XLA Ops:
  0.0 0.0 copy-start
  0.0 1.7 %copy-done = bf16[24,2,4,3,1,4,512]{6,5,4,3,2,1,0:T(4,128)(2,1)S(1)} copy-done((bf16[24,2,4,3,1,4,512]{6,5,4,3,2,1,0:T(4,128)(2,1)S(1)}, bf16[24,2,4,3,1,4,512]{6,5,4,3,2,1,0:T(4,128)(2,1)}, u32[]{:S(2)}) %copy-start) | copy-done | bytes 2359320
  1.7 0.0 copy-start.1
  1.7 1.1 %copy-done.1 = f32[1,192,768]{2,1,0:T(8,128)S(1)} copy-done((f32[1,192,768]{2,1,0:T(8,128)S(1)}, f32[1,192,768]{2,1,0:T(8,128)}, u32[]{:S(2)}) %copy-start.1) | copy-done | bytes 589848
  2.7 0.0 copy-start.2
  2.7 1.0 %copy-done.2 = bf16[4,2,3,3,1,4,512]{6,5,4,3,2,1,0:T(4,128)(2,1)S(1)} copy-done((bf16[4,2,3,3,1,4,512]{6,5,4,3,2,1,0:T(4,128)(2,1)S(1)}, bf16[4,2,3,3,1,4,512]{6,5,4,3,2,1,0:T(4,128)(2,1)}, u32[]{:S(2)}) %copy-start.2) | copy-done | bytes 294936
  3.7 0.0 copy-start.3
  3.7 0.9 %copy-done.3 = bf16[2,4,3,1,4,512]{5,4,3,2,1,0:T(4,128)(2,1)S(1)} copy-done((bf16[2,4,3,1,4,512]{5,4,3,2,1,0:T(4,128)(2,1)S(1)}, bf16[2,4,3,1,4,512]{5,4,3,2,1,0:T(4,128)(2,1)}, u32[]{:S(2)}) %copy-start.3) | copy-done | bytes 98328
  4.6 0.0 copy-start.4
  4.6 0.9 %copy-done.4 = f32[4,3,1,4,512]{4,3,2,1,0:T(4,128)S(1)} copy-done((f32[4,3,1,4,512]{4,3,2,1,0:T(4,128)S(1)}, f32[4,3,1,4,512]{4,3,2,1,0:T(4,128)}, u32[]{:S(2)}) %copy-start.4) | copy-done | bytes 98328
  5.5 0.0 copy-start.5
  5.5 0.7 %copy-done.5 = s32[1,4,512]{2,1,0:T(4,128)S(1)} copy-done((s32[1,4,512]{2,1,0:T(4,128)S(1)}, s32[1,4,512]{2,1,0:T(4,128)}, u32[]{:S(2)}) %copy-start.5) | copy-done | bytes 8216
  6.2 21.9 %shard_map.64 = f32[24,4,512]{2,1,0:T(4,128)S(1)} custom-call(bf16[24,4,512]{2,1,0:T(4,128)(2,1)S(1)} %bitcast.13, bf16[72,4,512]{2,1,0:T(4,128)(2,1)S(1)} %bitcast.12, f32[12,4,512]{2,1,0:T(4,128)S(1)} %bitcast.14, s32[4,512]{1,0:T(4,128)S(1)} %bitcast.15, bf16[576,4,512]{2,1,0:T(4,128)(2,1)S(1)} %bitcast.9, f32[192,768]{1,0:T(8,128)S(1)} %bitcast.11), custom_call_target="tpu_custom_call" | custom-call | flops 20000000 | bytes 4000000 | tf_op jit(solution)/shard_map/pallas_call | solution.py:454
  28.1 0.7 %copy.9 = f32[2,4,3,1,4,512]{5,4,3,2,1,0:T(4,128)} copy(f32[2,4,3,1,4,512]{5,4,3,2,1,0:T(4,128)S(1)} %bitcast.10) | data formatting | bytes 393216
Async XLA Ops:
  0.0 1.7 %copy-start = (bf16[24,2,4,3,1,4,512]{6,5,4,3,2,1,0:T(4,128)(2,1)S(1)}, bf16[24,2,4,3,1,4,512]{6,5,4,3,2,1,0:T(4,128)(2,1)}, u32[]{:S(2)}) copy-start(bf16[24,2,4,3,1,4,512]{6,5,4,3,2,1,0:T(4,128)(2,1)} %param.10) | copy-start | bytes 7077892
  1.7 1.1 %copy-start.1 = (f32[1,192,768]{2,1,0:T(8,128)S(1)}, f32[1,192,768]{2,1,0:T(8,128)}, u32[]{:S(2)}) copy-start(f32[1,192,768]{2,1,0:T(8,128)} %param.11) | copy-start | bytes 1769476
  2.7 1.0 %copy-start.2 = (bf16[4,2,3,3,1,4,512]{6,5,4,3,2,1,0:T(4,128)(2,1)S(1)}, bf16[4,2,3,3,1,4,512]{6,5,4,3,2,1,0:T(4,128)(2,1)}, u32[]{:S(2)}) copy-start(bf16[4,2,3,3,1,4,512]{6,5,4,3,2,1,0:T(4,128)(2,1)} %param.7) | copy-start | bytes 884740
  3.7 0.9 %copy-start.3 = (bf16[2,4,3,1,4,512]{5,4,3,2,1,0:T(4,128)(2,1)S(1)}, bf16[2,4,3,1,4,512]{5,4,3,2,1,0:T(4,128)(2,1)}, u32[]{:S(2)}) copy-start(bf16[2,4,3,1,4,512]{5,4,3,2,1,0:T(4,128)(2,1)} %param.6) | copy-start | bytes 294916
  4.6 0.9 %copy-start.4 = (f32[4,3,1,4,512]{4,3,2,1,0:T(4,128)S(1)}, f32[4,3,1,4,512]{4,3,2,1,0:T(4,128)}, u32[]{:S(2)}) copy-start(f32[4,3,1,4,512]{4,3,2,1,0:T(4,128)} %param.8) | copy-start | bytes 294916
  5.5 0.7 %copy-start.5 = (s32[1,4,512]{2,1,0:T(4,128)S(1)}, s32[1,4,512]{2,1,0:T(4,128)}, u32[]{:S(2)}) copy-start(s32[1,4,512]{2,1,0:T(4,128)} %param.9) | copy-start | bytes 24580

commit v2 on v1

--- a/solution.py
+++ b/solution.py
@@ -490,7 +490,7 @@
             dma((n_gz - 1,)),
         ],
         compiler_params=pltpu.CompilerParams(
-            collective_id=0, has_side_effects=True, vmem_limit_bytes=32 * 1024 * 1024
+            collective_id=0, has_side_effects=True, vmem_limit_bytes=60 * 1024 * 1024
         ),
         cost_estimate=pl.CostEstimate(flops=20000000, bytes_accessed=4000000, transcendentals=0),
     )(

time: 29.1 us -> 23.8 us (0.82)
  local copies, waits for them, and re-layouts: 6.85 us -> 1.62 us
    unnamed x13 -> x1, local copies, waits for them, and re-layouts: 6.85 us -> 1.62 us
where the time goes in v2:
time: 23.8 us; the launch traced here: 23.6 us
  Pallas kernels  22 us (92%)
  local copies, waits for them, and re-layouts  1.62 us (7%)
    pallas_call x1, Pallas kernels, shards(): pl.pallas_call(functools.partial(kernel, n_ta, n_gz, rows), out_shape=jax...  22 us
    unnamed x1, local copies, waits for them, and re-layouts  1.62 us

profile of v2, /device:TPU:0, one launch (start us, length us, event | category | flops | bytes accessed | tf_op | source)
XLA Modules:
  0.0 23.6 jit_solution(4343751323180968017)
XLA Ops:
  0.0 22.0 %shard_map.64 = f32[24,4,512]{2,1,0:T(4,128)} custom-call(bf16[24,4,512]{2,1,0:T(4,128)(2,1)} %bitcast.13, bf16[72,4,512]{2,1,0:T(4,128)(2,1)} %bitcast.12, f32[12,4,512]{2,1,0:T(4,128)} %bitcast.14, s32[4,512]{1,0:T(4,128)} %bitcast.15, bf16[576,4,512]{2,1,0:T(4,128)(2,1)} %bitcast.9, f32[192,768]{1,0:T(8,128)} %bitcast.11), custom_call_target="tpu_custom_call" | custom-call | flops 20000000 | bytes 4000000 | tf_op jit(solution)/shard_map/pallas_call | solution.py:454
  22.0 1.6 %copy.9 = f32[2,4,3,1,4,512]{5,4,3,2,1,0:T(4,128)} copy(f32[2,4,3,1,4,512]{5,4,3,2,1,0:T(4,128)} %bitcast.10) | data formatting | bytes 393216

commit v3 on v2

--- a/solution.py
+++ b/solution.py
@@ -211,8 +211,6 @@
             there = pl.ds(part * 12 + at, 3)
             field[there] = source[there] * inv
 
-    pl.semaphore_wait(barrier, 2 + n_gz - 1)
-
     def select(mask, first, second):
         return jnp.where(mask[None], first, second)
 
@@ -274,17 +272,27 @@
         ]
         fwd_t = stack_half(project(field, 3, -1))
         t_send[sweep, 0] = fwd_t.reshape(96, HALF).astype(BF16)
-        copies[0].start()
+        if sweep == 1:
+            copies[0].start()
         fwd_z = stack_half(project(field, 2, -1))
         z_send[sweep, 0] = pack_rows(fwd_z, 0)
-        copies[2].start()
+        if sweep == 1:
+            copies[2].start()
         before_links()
         back_t = stack_half(mix(links, 3, project(field, 3, 1), True))
         t_send[sweep, 1] = back_t.reshape(96, HALF).astype(BF16)
-        copies[1].start()
+        if sweep == 1:
+            copies[1].start()
         back_z = stack_half(mix(links, 2, project(field, 2, 1), True))
         z_send[sweep, 1] = pack_rows(back_z, 3)
-        copies[3].start()
+        if sweep == 1:
+            copies[3].start()
+
+        if sweep == 0:
+            beside()
+            pl.semaphore_wait(barrier, 2 + n_gz - 1)
+            for which in (1, 0, 3, 2):
+                copies[which].start()
 
         total[...] = jnp.zeros((NCOMP, 8, HALF), F32)
         for direction in range(2):
@@ -294,7 +302,8 @@
                 shift(direction, -1), mix(links, direction, project(field, direction, 1), True)
             )
             accumulate(total, behind, direction, 1)
-        beside()
+        if sweep == 1:
+            beside()
         for copy in copies:
             copy.wait()
         ahead_z = fill_rows(

time: 23.8 us -> 24.5 us (1.029)
  Pallas kernels: 22 us -> 22.7 us
    pallas_call x1, Pallas kernels: 22 us -> 22.7 us  [shards(): pl.pallas_call(functools.partial(kernel, n_ta, n_gz, rows), out_shape=jax...]
where the time goes in v3:
time: 24.5 us; the launch traced here: 24.4 us
  Pallas kernels  22.7 us (93%)
  local copies, waits for them, and re-layouts  1.62 us (7%)
    pallas_call x1, Pallas kernels, shards(): pl.pallas_call(functools.partial(kernel, n_ta, n_gz, rows), out_shape=jax...  22.7 us
    unnamed x1, local copies, waits for them, and re-layouts  1.62 us

profile of v3, /device:TPU:0, one launch (start us, length us, event | category | flops | bytes accessed | tf_op | source)
XLA Modules:
  0.0 24.4 jit_solution(1922585041058760072)
XLA Ops:
  0.0 22.7 %shard_map.64 = f32[24,4,512]{2,1,0:T(4,128)} custom-call(bf16[24,4,512]{2,1,0:T(4,128)(2,1)} %bitcast.13, bf16[72,4,512]{2,1,0:T(4,128)(2,1)} %bitcast.12, f32[12,4,512]{2,1,0:T(4,128)} %bitcast.14, s32[4,512]{1,0:T(4,128)} %bitcast.15, bf16[576,4,512]{2,1,0:T(4,128)(2,1)} %bitcast.9, f32[192,768]{1,0:T(8,128)} %bitcast.11), custom_call_target="tpu_custom_call" | custom-call | flops 20000000 | bytes 4000000 | tf_op jit(solution)/shard_map/pallas_call | solution.py:463
  22.7 1.6 %copy.9 = f32[2,4,3,1,4,512]{5,4,3,2,1,0:T(4,128)} copy(f32[2,4,3,1,4,512]{5,4,3,2,1,0:T(4,128)} %bitcast.10) | data formatting | bytes 393216

commit v4 on v2

--- a/solution.py
+++ b/solution.py
@@ -169,7 +169,7 @@
             )
         )
     ]
-    for load in loads:
+    for load in loads[:4]:
         load.start()
     load_source, load_clover, load_links, load_map, load_prolong, load_inverse = loads
 
@@ -313,6 +313,8 @@
 
     def widen_links():
         load_links.wait()
+        load_prolong.start()
+        load_inverse.start()
         for direction in (3, 2, 1, 0):
             for part in range(2):
                 for row in range(3):

time: 23.8 us -> 23.8 us (level)
  no operation moved by 1% of the time
where the time goes in v4:
time: 23.8 us; the launch traced here: 23.6 us
  Pallas kernels  22 us (92%)
  local copies, waits for them, and re-layouts  1.62 us (7%)
    pallas_call x1, Pallas kernels, shards(): pl.pallas_call(functools.partial(kernel, n_ta, n_gz, rows), out_shape=jax...  22 us
    unnamed x1, local copies, waits for them, and re-layouts  1.62 us

profile of v4, /device:TPU:0, one launch (start us, length us, event | category | flops | bytes accessed | tf_op | source)
XLA Modules:
  0.0 23.6 jit_solution(3584550885618303644)
XLA Ops:
  0.0 22.0 %shard_map.64 = f32[24,4,512]{2,1,0:T(4,128)} custom-call(bf16[24,4,512]{2,1,0:T(4,128)(2,1)} %bitcast.13, bf16[72,4,512]{2,1,0:T(4,128)(2,1)} %bitcast.12, f32[12,4,512]{2,1,0:T(4,128)} %bitcast.14, s32[4,512]{1,0:T(4,128)} %bitcast.15, bf16[576,4,512]{2,1,0:T(4,128)(2,1)} %bitcast.9, f32[192,768]{1,0:T(8,128)} %bitcast.11), custom_call_target="tpu_custom_call" | custom-call | flops 20000000 | bytes 4000000 | tf_op jit(solution)/shard_map/pallas_call | solution.py:456
  22.0 1.6 %copy.9 = f32[2,4,3,1,4,512]{5,4,3,2,1,0:T(4,128)} copy(f32[2,4,3,1,4,512]{5,4,3,2,1,0:T(4,128)} %bitcast.10) | data formatting | bytes 393216
